TPU v7x, 128 devices: a whole 4x4x4 slice. The times are simulated.
128 devices in a mesh: ctx: 32 (over z, x, y_hi), head: 4 (over y_lo, core).
Axes of the slice: x: 4, y: 4 (y_hi: 2, y_lo: 2; y = y_hi * 2 + y_lo), z: 4, core: 2. Of those that a mesh axis runs over, the one named last changes fastest.
Arguments:
- probe_vectors: bfloat16 [1024, 8192], P('ctx', 'head'), may hold values from -160 to 160
- lookup_tensor: bfloat16 [32768, 1024], P('ctx', 'head'), may hold values from -4.5 to 4.5
- payload_tensor: bfloat16 [32768, 1024], P('ctx', 'head'), may hold values from -6 to 6
- sequence_locations: int32 [1024], replicated, may hold values from 0 to 32767, as said below
- attention_return_matrix: bfloat16 [8192, 8192], P('head', 'ctx'), may hold values from -0.0625 to 0.0625
- skip_stream_state: bfloat16 [1024, 8192], P('head', 'ctx'), may hold values from -4 to 4
- early_rescaling_factor: float32 [8192], P('ctx'), may hold values from 0.5 to 1.5
- lexicon_projection_matrix: bfloat16 [8192, 65536], P(None, ('ctx', 'head')), may hold values from -0.1875 to 0.1875
- calibrating_divisor: float32 [1024], replicated, may hold values from 0.02 to 1
- desired_tokens_list: int32 [1024], replicated, may hold values from 0 to 65535
Outputs:
- hidden: bfloat16 [1024, 8192], P('head', 'ctx')
- logprob: float32 [1024], replicated
Inputs may be any that keep to these rules, and one draw needn't show every extreme that they name: `sequence_locations`: query i stands at a position from i * 32 to (i + 1) * 32 - 1; the last query stands at 32767.
All inputs are finite; a program needn't handle non-finite values.
Results may differ from a plain program's by a relative error of at most 0.0014.
The roundings to bfloat16 on the way count: a program that leaves them out, or rounds other values in their place, can miss the bound.
Values may be sent and summed in bfloat16 or wider, within the bound.
A program may use at most 192 MiB of HBM per device.

v0:
```python
import math
import jax
import jax.numpy as jnp
from jax import lax
from jax.sharding import Mesh
from jax.sharding import PartitionSpec as P

D = 8192
QUERY_HEAD_COUNT = 64
KEY_VALUE_HEADS = 8
HEAD_SIZE = 128
CTX = ("ctx_0", "ctx_1", "ctx_2")
HEAD = ("head_0", "head_1")
CTX_HEAD = ("ctx_0", "ctx_1", "ctx_2", "head_0", "head_1")
neg_big = -1e30
eps = 1e-05


def copy_for_each(x, axis):
    devices = lax.axis_size(axis)
    return lax.all_to_all(jnp.broadcast_to(x[None], (devices, *x.shape)), axis, 0, 0, tiled=True)


def taken_together(x, axis):
    everything = copy_for_each(x, axis)
    return jnp.max(everything, axis=0)


def sent_together(arrays, axis, dim, along):
    widths = [math.prod(a.shape[along:]) for a in arrays]
    both = jnp.concatenate(
        [a.reshape(*a.shape[:along], w) for a, w in zip(arrays, widths)], axis=along
    )
    result = lax.psum_scatter(both, axis, scatter_dimension=dim, tiled=True)
    tiles = jnp.split(result, [sum(widths[:k]) for k in range(1, len(widths))], axis=along)
    return tuple(
        (b.reshape(*result.shape[:along], *a.shape[along:]) for a, b in zip(arrays, tiles))
    )


def in_blocks(x, dim, devices):
    shape = x.shape
    tiles = x.reshape(*shape[:dim], devices, shape[dim] // devices, *shape[dim + 1 :])
    return jnp.moveaxis(tiles, dim, 0)


def sent_and_summed(x, axis, dim):
    devices = lax.axis_size(axis)
    tiles = lax.all_to_all(in_blocks(x, dim, devices), axis, 0, 0, tiled=True)
    return jnp.sum(tiles, axis=0)


def of_everyone(x, axis):
    everything = copy_for_each(x, axis)
    return jnp.sum(everything, axis=0)


def collected_together(x, axis):
    leaves = jax.tree.leaves(x)
    sequence = sorted(range(len(leaves)), key=lambda k: -leaves[k].size)
    width = (1, *leaves[sequence[0]].shape)[-1]
    lines = [
        jnp.pad(leaves[k].reshape(-1), (0, -leaves[k].size % width)).reshape(-1, width)
        for k in sequence
    ]
    both, at, found = (lax.all_gather(jnp.concatenate(lines), axis), 0, {})
    for k, line in zip(sequence, lines):
        slab = both[:, at : at + len(line)].reshape(len(both), -1)
        found[k] = slab[:, : leaves[k].size].reshape(-1, *leaves[k].shape)
        at += len(line)
    numbers = iter(range(len(leaves)))
    return jax.tree.map(lambda _: found[next(numbers)], x)


def joined_all(x, axes, combine):
    for axis in axes:
        pieces = collected_together(x, axis)
        x = jax.tree.map(lambda part: part[0], pieces)
        for k in range(1, lax.axis_size(axis)):
            x = combine(x, jax.tree.map(lambda part: part[k], pieces))
    return x


def unite_vocab(first, second):
    peak_first, total_first, picked_first = first
    peak_second, total_second, picked_second = second
    joined = jnp.maximum(peak_first, peak_second)
    total = total_first * jnp.exp(peak_first - joined) + total_second * jnp.exp(
        peak_second - joined
    )
    return (joined, total, picked_first + picked_second)


def local_attention(every_query, lookup_tensor, payload_tensor, sequence_locations, key_start):
    total_rows = every_query.shape[0]
    ctx_len = lookup_tensor.shape[0]
    kv_here = lookup_tensor.shape[1] // HEAD_SIZE
    group_size = QUERY_HEAD_COUNT // KEY_VALUE_HEADS
    scale_factor = HEAD_SIZE ** (-0.5)
    row_block = min(512, total_rows)
    query_heads = every_query.reshape(total_rows, kv_here, group_size, HEAD_SIZE)
    key_heads = lookup_tensor.reshape(ctx_len, kv_here, HEAD_SIZE)
    value_heads = payload_tensor.reshape(ctx_len, kv_here, HEAD_SIZE)
    key_pos = key_start + jnp.arange(ctx_len, dtype=jnp.int32)
    maxima, sums, accums = ([], [], [])
    for row_start in range(0, total_rows, row_block):
        row_pos = sequence_locations[row_start : row_start + row_block]
        visible = key_pos[None, None, :] <= row_pos[:, None, None]
        head_max, head_sum, head_acc = ([], [], [])
        for kv_head in range(kv_here):
            scores = (
                jnp.einsum(
                    "qhd,kd->qhk",
                    query_heads[row_start : row_start + row_block, kv_head],
                    key_heads[:, kv_head],
                    preferred_element_type=jnp.float32,
                )
                * scale_factor
            )
            block_max = jnp.max(jnp.where(visible, scores, neg_big), axis=-1)
            weights = jnp.where(visible, jnp.exp(scores - block_max[..., None]), 0.0)
            head_sum.append(jnp.sum(weights, axis=-1))
            head_max.append(block_max)
            head_acc.append(
                jnp.einsum(
                    "qhk,kd->qhd",
                    weights.astype(jnp.bfloat16),
                    value_heads[:, kv_head],
                    preferred_element_type=jnp.float32,
                )
            )
        maxima.append(jnp.concatenate(head_max, axis=1))
        sums.append(jnp.concatenate(head_sum, axis=1))
        accums.append(jnp.concatenate(head_acc, axis=1))
    return (
        jnp.concatenate(maxima, axis=0),
        jnp.concatenate(sums, axis=0),
        jnp.concatenate(accums, axis=0),
    )


def shards(
    probe_vectors,
    lookup_tensor,
    payload_tensor,
    sequence_locations,
    attention_return_matrix,
    skip_stream_state,
    early_rescaling_factor,
    lexicon_projection_matrix,
    calibrating_divisor,
    desired_tokens_list,
):
    heads_here = probe_vectors.shape[1] // HEAD_SIZE
    every_query = lax.all_gather(probe_vectors, CTX, axis=0, tiled=True)
    key_start = lax.axis_index(CTX) * lookup_tensor.shape[0]
    local_max, local_sum, local_acc = local_attention(
        every_query, lookup_tensor, payload_tensor, sequence_locations, key_start
    )
    global_max = taken_together(local_max.astype(jnp.bfloat16), CTX).astype(local_max.dtype)
    rescale = jnp.exp(local_max - global_max)
    acc_rows, sum_rows = sent_together(
        (local_acc * rescale[..., None], local_sum * rescale), CTX, 0, 2
    )
    attn = (
        (acc_rows / sum_rows[..., None])
        .astype(jnp.bfloat16)
        .reshape(acc_rows.shape[0], heads_here * HEAD_SIZE)
    )
    mixed_part = jnp.dot(
        lax.all_gather(attn, CTX, axis=0, tiled=True),
        attention_return_matrix,
        preferred_element_type=jnp.float32,
    )
    mixed_rows = sent_and_summed(mixed_part, HEAD, 0)
    hidden = (skip_stream_state.astype(jnp.float32) + mixed_rows).astype(jnp.bfloat16)
    widened = hidden.astype(jnp.float32)
    square_total = of_everyone(jnp.sum(widened * widened, axis=1), CTX)
    normed = (
        widened * lax.rsqrt(square_total / D + eps)[:, None] * early_rescaling_factor[None, :]
    ).astype(jnp.bfloat16)
    full_rows = lax.all_gather(normed, CTX, axis=1, tiled=True)
    early_class_energies = jnp.dot(
        lax.all_gather(full_rows, HEAD, axis=0, tiled=True),
        lexicon_projection_matrix,
        preferred_element_type=jnp.float32,
    )
    tempered_affinities = early_class_energies / calibrating_divisor[:, None]
    vocab_here = lexicon_projection_matrix.shape[1]
    offset = (lax.axis_index(CTX) * lax.axis_size(HEAD) + lax.axis_index(HEAD)) * vocab_here
    column_ids = jnp.arange(vocab_here, dtype=jnp.int32)[None, :] + offset
    picked = jnp.sum(
        jnp.where(column_ids == desired_tokens_list[:, None], tempered_affinities, 0.0), axis=1
    )
    local_peak = jnp.max(tempered_affinities, axis=1)
    local_total = jnp.sum(jnp.exp(tempered_affinities - local_peak[:, None]), axis=1)
    peak, total, target_logit = joined_all((local_peak, local_total, picked), CTX_HEAD, unite_vocab)
    logprob = target_logit - peak - jnp.log(total)
    return (hidden, logprob)


def solution(mesh):
    torus = Mesh(
        mesh.devices.reshape(4, 4, 2, 2, 2), ("ctx_0", "ctx_1", "ctx_2", "head_0", "head_1")
    )
    placed = (
        P(CTX, HEAD),
        P(CTX, HEAD),
        P(CTX, HEAD),
        P(),
        P(HEAD, CTX),
        P(HEAD, CTX),
        P(CTX),
        P(None, CTX_HEAD),
        P(),
        P(),
    )
    return jax.shard_map(
        shards, mesh=torus, in_specs=placed, out_specs=(P(HEAD, CTX), P()), check_vma=False
    )
```

profile of v0, /device:TPU:1, one launch (start us, length us, event | category | flops | bytes accessed | tf_op | source)
XLA Modules:
  0.0 1000.2 jit_solution(12280744665633798866)
XLA Ops:
  7.2 0.0 copy-start
  7.2 0.0 all-gather.15.cloned.1.call-start
  7.2 0.7 all-gather.15.cloned.1.call-update
  7.9 1.2 copy.117
  9.2 1.2 copy.119
  10.5 0.8 fusion.82
  11.2 0.7 broadcast_compare_fusion.1
  11.9 82.4 %all-gather.15.cloned.1.call-done = bf16[1024,2048]{1,0:T(8,128)(2,1)} async-done(((bf16[32,2048]{1,0:T(8,128)(2,1)}), bf16[1024,2048]{1,0:T(8,128)(2,1)}) %all-gather.15.cloned.1.call-update) | async-done | bytes 4194320 | tf_op jit(solution)/shard_map/all_gather | solution.py:155
  94.2 6.4 copy.115
  100.6 8.8 select_reduce_fusion.3
  109.4 0.0 copy-done.3
  109.4 15.3 %fusion = (f32[512,8]{0,1:T(8,128)S(1)}, f32[512,8]{0,1:T(8,128)S(1)}, f32[512,8,1024]{2,0,1:T(8,128)}) fusion(f32[512,8,1024]{2,0,1:T(8,128)} %get-tuple-element.31, f32[512,8]{0,1:T(8,128)S(1)} %get-tuple-element.30, pred[512,1024]{1,0:T(8,128)(4,1)S(1)} %get-tuple-element.23, bf16[1024,2,128]{0,2,1:T(8,128)(2,1)S(1)} %bitcast.321, ...), kind=kOutput, calls=%fused_computation.9 | convolution fusion | flops 1103093760 | bytes 35438592 | tf_op jit(solution)/shard_map/qhd,kd->qhk/dot_general | solution.py:112
  124.7 8.5 fusion.14
  133.1 7.4 select_reduce_fusion.1
  140.6 8.5 fusion.10
  149.0 15.3 %fusion.4 = (f32[512,8]{0,1:T(8,128)S(1)}, f32[512,8]{0,1:T(8,128)S(1)}, f32[512,8,1024]{2,0,1:T(8,128)}) fusion(f32[512,8,1024]{2,0,1:T(8,128)} %get-tuple-element.28, f32[512,8]{0,1:T(8,128)S(1)} %get-tuple-element.27, pred[512,1024]{1,0:T(8,128)(4,1)S(1)} %get-tuple-element.24, bf16[1024,2,128]{0,2,1:T(8,128)(2,1)S(1)} %bitcast.323, ...), kind=kOutput, calls=%fused_computation.13 | convolution fusion | flops 1103093760 | bytes 35438592 | tf_op jit(solution)/shard_map/qhd,kd->qhk/dot_general | solution.py:112
  164.3 8.8 fusion.12
  173.1 2.5 copy-done.2
  175.6 11.1 %fusion.2 = (f32[512,8]{0,1:T(8,128)S(1)}, f32[512,8]{0,1:T(8,128)S(1)}) fusion(f32[512,8,1024]{2,0,1:T(8,128)} %get-tuple-element.32, f32[512,8]{0,1:T(8,128)S(1)} %get-tuple-element.5, pred[512,1024]{1,0:T(8,128)(4,1)S(1)} %get-tuple-element.23, f32[512,8]{0,1:T(8,128)S(1)} %get-tuple-element.7, f32[512,8,1024]{2,0,1:T(8,128)S(1)} %copy-done.2, ...), kind=kLoop, calls=%fused_computation.11 | loop fusion | flops 33546240 | bytes 34668544 | tf_op jit(solution)/shard_map/reduce_sum | solution.py:122
  186.7 1.1 broadcast_in_dim.79
  187.8 5.3 all-to-all-start
  193.1 0.0 reduce-scatter.2.cloned.1.call-start
  193.1 8.5 fusion.8
  201.6 9.5 all-to-all-done
  211.1 0.2 reduce_max.58
  211.3 4.7 copy.126
  216.0 6.4 maximum_multiply_fusion
  222.5 0.0 copy-done.1
  222.5 6.1 pad_maximum_fusion
  228.5 0.0 reduce-scatter.2.cloned.1.call-update
  228.6 0.0 all-gather.17.cloned.1.call-start
  228.6 357.1 %reduce-scatter.2.cloned.1.call-done = f32[32,16,129]{2,0,1:T(8,128)} async-done(((f32[1024,16,129]{2,0,1:T(8,128)}), f32[32,16,129]{2,0,1:T(8,128)}) %reduce-scatter.2.cloned.1.call-update) | async-done | bytes 264208 | tf_op jit(solution)/shard_map/reduce_scatter | solution.py:34
  585.7 1.1 slice_reduce_fusion
  586.8 1.7 copy_bitcast_fusion
  588.6 0.0 all-gather.17.cloned.1.call-update
  588.6 0.0 all-gather.19.cloned.1.call-start
  588.7 84.5 %all-gather.17.cloned.1.call-done = bf16[1024,2048]{1,0:T(8,128)(2,1)} async-done(((bf16[32,2048]{1,0:T(8,128)(2,1)}), bf16[1024,2048]{1,0:T(8,128)(2,1)}) %all-gather.17.cloned.1.call-update) | async-done | bytes 4194320 | tf_op jit(solution)/shard_map/all_gather | solution.py:171
  673.2 0.0 copy-done
  673.2 3.4 fusion.84
  676.6 16.9 %all_to_all.16 = f32[4,256,256]{2,1,0:T(8,128)S(1)} all-to-all(f32[4,256,256]{2,1,0:T(8,128)S(1)} %bitcast.315), channel_id=1, replica_groups=mesh['ctx_0'=4,'ctx_1'=4,'ctx_2'=2,'head_0'=2,'head_1'=2] {'head_0','hea..., dimensions={0} | all-to-all | bytes 2097152 | tf_op jit(solution)/shard_map/all_to_all | solution.py:49
  693.5 0.1 reduce_sum.85
  693.6 0.0 copy-done.5
  693.6 0.1 fusion.24
  693.8 14.4 %all_to_all.17 = f32[32,1,256]{2,1,0:T(1,128)S(1)} all-to-all(f32[32,1,256]{2,1,0:T(1,128)S(1)} %broadcast_in_dim.80), channel_id=1, replica_groups=mesh['ctx_0'=4,'ctx_1'=4,'ctx_2'=2,'head_0'=2,'head_1'=2] {'ctx_0','ctx_..., dimensions={0} | all-to-all | bytes 65536 | tf_op jit(solution)/shard_map/all_to_all | solution.py:21
  708.2 0.1 reduce_sum.87
  708.2 0.7 fusion.26
  709.0 0.0 all-gather.19.cloned.1.call-update
  709.0 0.0 all-gather.21.cloned.1.call-start
  709.0 77.2 %all-gather.19.cloned.1.call-done = bf16[256,8192]{1,0:T(8,128)(2,1)} async-done(((bf16[256,256]{1,0:T(8,128)(2,1)}), bf16[256,8192]{1,0:T(8,128)(2,1)}) %all-gather.19.cloned.1.call-update) | async-done | bytes 4194320 | tf_op jit(solution)/shard_map/all_gather | solution.py:182
  786.2 0.0 all-gather.21.cloned.1.call-update
  786.3 0.0 copy-start.6
  786.3 153.9 %all-gather.21.cloned.1.call-done = bf16[1024,8192]{1,0:T(8,128)(2,1)} async-done(((bf16[256,8192]{1,0:T(8,128)(2,1)}), bf16[1024,8192]{1,0:T(8,128)(2,1)}) %all-gather.21.cloned.1.call-update) | async-done | bytes 16777232 | tf_op jit(solution)/shard_map/all_gather | solution.py:184
  940.2 17.1 %fusion.83 = (f32[1024]{0:T(1024)S(1)}, f32[1024,512]{0,1:T(8,128)S(1)}) fusion(f32[1024]{0:T(1024)S(1)} %copy-done.8, bf16[1024,8192]{1,0:T(8,128)(2,1)} %all-gather.21.cloned.1.call-done, bf16[8192,512]{1,0:T(8,128)(2,1)} %param.17), kind=kOutput, calls=%fused_computation.154 | convolution fusion | flops 8590982144 | bytes 27271168 | tf_op jit(solution)/shard_map/dot_general | solution.py:183
  957.3 0.0 copy-done.4
  957.3 0.0 copy-done.6
  957.3 0.5 exponential_reduce_fusion
  957.8 9.7 all-gather.5
  967.5 0.1 fusion.54
  967.6 9.3 all-gather.6
  976.9 0.1 fusion.44
  977.0 4.8 all-gather.7
  981.8 3.3 all-gather.8
  985.1 7.9 all-gather.9
  993.1 0.6 log_subtract_fusion
  (31 shorter events, 0.3 us)
Async XLA Ops:
  7.2 666.0 %copy-start = (bf16[2048,256]{1,0:T(8,128)(2,1)S(1)}, bf16[2048,256]{1,0:T(8,128)(2,1)}, u32[]{:S(2)}) copy-start(bf16[2048,256]{1,0:T(8,128)(2,1)} %param.14) | copy-start | bytes 3145732
  7.2 87.1 %all-gather.15.cloned.1.call-start = ((), (), s32[]{:S(2)}) async-start(), calls=%async_computation.4 | async-start | bytes 4325376 | tf_op jit(solution)/shard_map/all_gather | solution.py:155
  100.6 8.8 copy-start.3
  164.3 11.3 %copy-start.2 = (f32[512,8,1024]{2,0,1:T(8,128)S(1)}, f32[512,8,1024]{2,0,1:T(8,128)}, u32[]{:S(2)}) copy-start(f32[512,8,1024]{2,0,1:T(8,128)} %get-tuple-element.29) | copy-start | bytes 50331652
  187.8 23.3 %all-to-all-start = ((bf16[32,1024,16]{1,2,0:T(8,128)(2,1)}), bf16[32,1024,16]{1,2,0:T(8,128)(2,1)S(1)}, u32[]{:S(2)}, u32[]{:S(2)}) async-start(bf16[32,1024,16]{1,2,0:T(8,128)(2,1)} %broadcast_in_dim.79), calls=%async_computation | async-start | bytes 2097152 | tf_op jit(solution)/shard_map/all_to_all | solution.py:21
  193.1 392.7 %reduce-scatter.2.cloned.1.call-start = ((), (), s32[]{:S(2)}) async-start(), calls=%async_computation.5 | async-start | bytes 17301504 | tf_op jit(solution)/shard_map/reduce_scatter | solution.py:34
  216.0 6.4 copy-start.1
  228.5 465.1 %copy-start.5 = (bf16[256,256]{1,0:T(8,128)(2,1)S(1)}, bf16[256,256]{1,0:T(8,128)(2,1)}, u32[]{:S(2)}) copy-start(bf16[256,256]{1,0:T(8,128)(2,1)} %param.15) | copy-start | bytes 393220
  228.5 479.7 %copy-start.7 = (f32[256]{0:T(256)S(1)}, f32[256]{0:T(256)}, u32[]{:S(2)}) copy-start(f32[256]{0:T(256)} %param.16) | copy-start | bytes 3076
  228.5 711.7 %copy-start.8 = (f32[1024]{0:T(1024)S(1)}, f32[1024]{0:T(1024)}, u32[]{:S(2)}) copy-start(f32[1024]{0:T(1024)} %param.18) | copy-start | bytes 12292
  228.6 444.6 %all-gather.17.cloned.1.call-start = ((), (), s32[]{:S(2)}) async-start(), calls=%async_computation.6 | async-start | bytes 4325376 | tf_op jit(solution)/shard_map/all_gather | solution.py:171
  588.6 197.6 %all-gather.19.cloned.1.call-start = ((), (), s32[]{:S(2)}) async-start(), calls=%async_computation.7 | async-start | bytes 4325376 | tf_op jit(solution)/shard_map/all_gather | solution.py:182
  693.7 263.5 %copy-start.4 = (bf16[256,256]{1,0:T(8,128)(2,1)}, bf16[256,256]{1,0:T(8,128)(2,1)S(1)}, u32[]{:S(2)}) copy-start(bf16[256,256]{1,0:T(8,128)(2,1)S(1)} %get-tuple-element.17) | copy-start | bytes 393220
  709.0 231.2 %all-gather.21.cloned.1.call-start = ((), (), s32[]{:S(2)}) async-start(), calls=%async_computation.8 | async-start | bytes 20971520 | tf_op jit(solution)/shard_map/all_gather | solution.py:184
  786.3 171.0 %copy-start.6 = (s32[1024]{0:T(1024)S(1)}, s32[1024]{0:T(1024)}, u32[]{:S(2)}) copy-start(s32[1024]{0:T(1024)} %param.19) | copy-start | bytes 12292
Sparse Core Ops, SparseCore 0:
  11.1 83.0 all-gather.14
  228.7 357.0 reduce-scatter.1
  589.4 83.7 all-gather.16
  709.1 77.0 all-gather.18
  787.7 152.3 all-gather.20
where the time goes:
time: 1000 us
  waiting for transfers between devices  765 us (76%)
  matrix products  101 us (10%)
  blocking collectives  66.2 us (7%)
  other arithmetic  28.6 us (3%)
  local copies, waits for them, and re-layouts  19.1 us (2%)
  between operations  14.1 us (1%)
    reduce_scatter x1, waiting for transfers between devices, sent_together(): result = lax.psum_scatter(both, axis, scatter_dimension=dim, tiled=True)  357 us
    all_gather x1, waiting for transfers between devices, shards(): lax.all_gather(full_rows, HEAD, axis=0, tiled=True)  154 us
    all_gather x1, waiting for transfers between devices, shards(): lax.all_gather(attn, CTX, axis=0, tiled=True)  84.5 us
    all_gather x1, waiting for transfers between devices, shards(): every_query = lax.all_gather(probe_vectors, CTX, axis=0, tiled=True)  82.4 us
    all_gather x1, waiting for transfers between devices, shards(): full_rows = lax.all_gather(normed, CTX, axis=1, tiled=True)  77.2 us
    dot_general x4, matrix products, local_attention(): jnp.einsum('qhd,kd->qhk', query_heads[row_start:row_start + row_block, kv...  46.7 us
    all_gather x5, blocking collectives, collected_together(): both, at, found = (lax.all_gather(jnp.concatenate(lines), axis), 0, {})  34.9 us
    dot_general x4, matrix products, local_attention(): jnp.einsum('qhk,kd->qhd', weights.astype(jnp.bfloat16), value_heads[:, kv...  34.2 us
  transfers between devices with their start and end apart: 6, of which 6 were waited for; matrix products, arithmetic and copies ran while one was open for 1% of the time, Pallas kernels for 0%

commit v1 on v0

--- a/solution.py
+++ b/solution.py
@@ -181,7 +181,9 @@
     ).astype(jnp.bfloat16)
     full_rows = lax.all_gather(normed, CTX, axis=1, tiled=True)
     early_class_energies = jnp.dot(
-        lax.all_gather(full_rows, HEAD, axis=0, tiled=True),
+        jnp.concatenate(
+            lax.all_to_all(jnp.stack([full_rows] * lax.axis_size(HEAD)), HEAD, 0, 0), axis=0
+        ),
         lexicon_projection_matrix,
         preferred_element_type=jnp.float32,
     )

time: 1000 us -> 1050 us (1.050)
  waiting for transfers between devices: 765 us -> 794 us
    all_to_all x0 -> x1, waiting for transfers between devices: none -> 182 us  [shards(): lax.all_to_all(jnp.stack([full_rows] * lax.axis_size(HEAD)), HEAD, 0, 0)]
    all_gather x1 -> x0, waiting for transfers between devices: 154 us -> none  [shards(): lax.all_gather(full_rows, HEAD, axis=0, tiled=True)]
where the time goes in v1:
time: 1050 us
  waiting for transfers between devices  794 us (76%)
  matrix products  101 us (10%)
  blocking collectives  68 us (6%)
  other arithmetic  28.6 us (3%)
  local copies, waits for them, and re-layouts  26.5 us (3%)
  between operations  14.1 us (1%)
  starting transfers between devices  13.6 us (1%)
    reduce_scatter x1, waiting for transfers between devices, sent_together(): result = lax.psum_scatter(both, axis, scatter_dimension=dim, tiled=True)  357 us
    all_to_all x1, waiting for transfers between devices, shards(): lax.all_to_all(jnp.stack([full_rows] * lax.axis_size(HEAD)), HEAD, 0, 0)  182 us
    all_gather x1, waiting for transfers between devices, shards(): lax.all_gather(attn, CTX, axis=0, tiled=True)  84.5 us
    all_gather x1, waiting for transfers between devices, shards(): every_query = lax.all_gather(probe_vectors, CTX, axis=0, tiled=True)  82.4 us
    all_gather x1, waiting for transfers between devices, shards(): full_rows = lax.all_gather(normed, CTX, axis=1, tiled=True)  77.2 us
    dot_general x4, matrix products, local_attention(): jnp.einsum('qhd,kd->qhk', query_heads[row_start:row_start + row_block, kv...  46.7 us
    all_gather x5, blocking collectives, collected_together(): both, at, found = (lax.all_gather(jnp.concatenate(lines), axis), 0, {})  36.7 us
    dot_general x4, matrix products, local_attention(): jnp.einsum('qhk,kd->qhd', weights.astype(jnp.bfloat16), value_heads[:, kv...  34.2 us
  transfers between devices with their start and end apart: 6, of which 6 were waited for; matrix products, arithmetic and copies ran while one was open for 1% of the time, Pallas kernels for 0%

profile of v1, /device:TPU:1, one launch (start us, length us, event | category | flops | bytes accessed | tf_op | source)
XLA Modules:
  0.0 1045.9 jit_solution(4295486074697829829)
XLA Ops:
  7.2 0.0 copy-start
  7.2 0.0 all-gather.14.cloned.1.call-start
  7.2 0.7 all-gather.14.cloned.1.call-update
  7.9 1.2 copy.117
  9.2 1.2 copy.119
  10.5 0.8 fusion.82
  11.2 0.7 broadcast_compare_fusion.1
  11.9 82.4 %all-gather.14.cloned.1.call-done = bf16[1024,2048]{1,0:T(8,128)(2,1)} async-done(((bf16[32,2048]{1,0:T(8,128)(2,1)}), bf16[1024,2048]{1,0:T(8,128)(2,1)}) %all-gather.14.cloned.1.call-update) | async-done | bytes 4194320 | tf_op jit(solution)/shard_map/all_gather | solution.py:155
  94.2 6.4 copy.115
  100.6 8.8 select_reduce_fusion.3
  109.4 0.0 copy-done.3
  109.4 15.3 %fusion = (f32[512,8]{0,1:T(8,128)S(1)}, f32[512,8]{0,1:T(8,128)S(1)}, f32[512,8,1024]{2,0,1:T(8,128)}) fusion(f32[512,8,1024]{2,0,1:T(8,128)} %get-tuple-element.31, f32[512,8]{0,1:T(8,128)S(1)} %get-tuple-element.30, pred[512,1024]{1,0:T(8,128)(4,1)S(1)} %get-tuple-element.23, bf16[1024,2,128]{0,2,1:T(8,128)(2,1)S(1)} %bitcast.322, ...), kind=kOutput, calls=%fused_computation.9 | convolution fusion | flops 1103093760 | bytes 35438592 | tf_op jit(solution)/shard_map/qhd,kd->qhk/dot_general | solution.py:112
  124.7 8.5 fusion.14
  133.1 7.4 select_reduce_fusion.1
  140.6 8.5 fusion.10
  149.0 15.3 %fusion.4 = (f32[512,8]{0,1:T(8,128)S(1)}, f32[512,8]{0,1:T(8,128)S(1)}, f32[512,8,1024]{2,0,1:T(8,128)}) fusion(f32[512,8,1024]{2,0,1:T(8,128)} %get-tuple-element.28, f32[512,8]{0,1:T(8,128)S(1)} %get-tuple-element.27, pred[512,1024]{1,0:T(8,128)(4,1)S(1)} %get-tuple-element.24, bf16[1024,2,128]{0,2,1:T(8,128)(2,1)S(1)} %bitcast.324, ...), kind=kOutput, calls=%fused_computation.13 | convolution fusion | flops 1103093760 | bytes 35438592 | tf_op jit(solution)/shard_map/qhd,kd->qhk/dot_general | solution.py:112
  164.3 8.8 fusion.12
  173.1 2.5 copy-done.2
  175.6 11.1 %fusion.2 = (f32[512,8]{0,1:T(8,128)S(1)}, f32[512,8]{0,1:T(8,128)S(1)}) fusion(f32[512,8,1024]{2,0,1:T(8,128)} %get-tuple-element.32, f32[512,8]{0,1:T(8,128)S(1)} %get-tuple-element.5, pred[512,1024]{1,0:T(8,128)(4,1)S(1)} %get-tuple-element.23, f32[512,8]{0,1:T(8,128)S(1)} %get-tuple-element.7, f32[512,8,1024]{2,0,1:T(8,128)S(1)} %copy-done.2, ...), kind=kLoop, calls=%fused_computation.11 | loop fusion | flops 33546240 | bytes 34668544 | tf_op jit(solution)/shard_map/reduce_sum | solution.py:122
  186.7 1.1 broadcast_in_dim.79
  187.8 5.3 all-to-all-start
  193.1 0.0 reduce-scatter.2.cloned.1.call-start
  193.1 8.5 fusion.8
  201.6 9.5 all-to-all-done
  211.1 0.2 reduce_max.58
  211.3 4.7 copy.126
  216.0 6.4 maximum_multiply_fusion
  222.5 0.0 copy-done.1
  222.5 6.1 pad_maximum_fusion
  228.5 0.0 reduce-scatter.2.cloned.1.call-update
  228.6 0.0 all-gather.16.cloned.1.call-start
  228.6 357.1 %reduce-scatter.2.cloned.1.call-done = f32[32,16,129]{2,0,1:T(8,128)} async-done(((f32[1024,16,129]{2,0,1:T(8,128)}), f32[32,16,129]{2,0,1:T(8,128)}) %reduce-scatter.2.cloned.1.call-update) | async-done | bytes 264208 | tf_op jit(solution)/shard_map/reduce_scatter | solution.py:34
  585.7 1.1 slice_reduce_fusion
  586.8 1.7 copy_bitcast_fusion
  588.6 0.0 all-gather.16.cloned.1.call-update
  588.6 0.0 all-gather.18.cloned.1.call-start
  588.7 84.5 %all-gather.16.cloned.1.call-done = bf16[1024,2048]{1,0:T(8,128)(2,1)} async-done(((bf16[32,2048]{1,0:T(8,128)(2,1)}), bf16[1024,2048]{1,0:T(8,128)(2,1)}) %all-gather.16.cloned.1.call-update) | async-done | bytes 4194320 | tf_op jit(solution)/shard_map/all_gather | solution.py:171
  673.2 0.0 copy-done
  673.2 3.4 fusion.84
  676.6 16.9 %all_to_all.21 = f32[4,256,256]{2,1,0:T(8,128)S(1)} all-to-all(f32[4,256,256]{2,1,0:T(8,128)S(1)} %bitcast.316), channel_id=1, replica_groups=mesh['ctx_0'=4,'ctx_1'=4,'ctx_2'=2,'head_0'=2,'head_1'=2] {'head_0','hea..., dimensions={0} | all-to-all | bytes 2097152 | tf_op jit(solution)/shard_map/all_to_all | solution.py:49
  693.5 0.1 reduce_sum.85
  693.6 0.0 copy-done.5
  693.6 0.1 fusion.24
  693.7 0.0 copy-start.4
  693.8 14.4 %all_to_all.22 = f32[32,1,256]{2,1,0:T(1,128)S(1)} all-to-all(f32[32,1,256]{2,1,0:T(1,128)S(1)} %broadcast_in_dim.80), channel_id=1, replica_groups=mesh['ctx_0'=4,'ctx_1'=4,'ctx_2'=2,'head_0'=2,'head_1'=2] {'ctx_0','ctx_..., dimensions={0} | all-to-all | bytes 65536 | tf_op jit(solution)/shard_map/all_to_all | solution.py:21
  708.1 0.1 reduce_sum.87
  708.2 0.0 copy-done.7
  708.2 0.7 fusion.26
  709.0 0.0 all-gather.18.cloned.1.call-update
  709.0 77.2 %all-gather.18.cloned.1.call-done = bf16[256,8192]{1,0:T(8,128)(2,1)} async-done(((bf16[256,256]{1,0:T(8,128)(2,1)}), bf16[256,8192]{1,0:T(8,128)(2,1)}) %all-gather.18.cloned.1.call-update) | async-done | bytes 4194320 | tf_op jit(solution)/shard_map/all_gather | solution.py:182
  786.2 7.4 stack.2
  793.6 0.0 copy-done.4
  793.6 8.1 all-to-all-start.3
  801.8 182.2 %all-to-all-done.3 = bf16[4,256,8192]{2,1,0:T(8,128)(2,1)} async-done(((bf16[4,256,8192]{2,1,0:T(8,128)(2,1)}), bf16[4,256,8192]{2,1,0:T(8,128)(2,1)}, u32[]{:S(2)}, u32[]{:S(2)}) %all-to-all-start.3) | async-done | bytes 16777248 | tf_op jit(solution)/shard_map/all_to_all | solution.py:185
  984.0 17.1 %fusion.83 = (f32[1024]{0:T(1024)S(1)}, f32[1024,512]{0,1:T(8,128)S(1)}) fusion(f32[1024]{0:T(1024)S(1)} %copy-done.8, bf16[1024,8192]{1,0:T(8,128)(2,1)} %bitcast.21, bf16[8192,512]{1,0:T(8,128)(2,1)} %param.17), kind=kOutput, calls=%fused_computation.154 | convolution fusion | flops 8590982144 | bytes 27271168 | tf_op jit(solution)/shard_map/dot_general | solution.py:183
  1001.1 0.5 exponential_reduce_fusion
  1001.6 9.1 all-gather.5
  1010.8 0.1 fusion.54
  1010.9 9.3 all-gather.6
  1020.2 0.1 fusion.44
  1020.3 4.8 all-gather.7
  1025.1 3.3 all-gather.8
  1028.4 10.3 all-gather.9
  1038.7 0.6 log_subtract_fusion
  (31 shorter events, 0.3 us)
Async XLA Ops:
  7.2 666.0 %copy-start = (bf16[2048,256]{1,0:T(8,128)(2,1)S(1)}, bf16[2048,256]{1,0:T(8,128)(2,1)}, u32[]{:S(2)}) copy-start(bf16[2048,256]{1,0:T(8,128)(2,1)} %param.14) | copy-start | bytes 3145732
  7.2 87.1 %all-gather.14.cloned.1.call-start = ((), (), s32[]{:S(2)}) async-start(), calls=%async_computation.5 | async-start | bytes 4325376 | tf_op jit(solution)/shard_map/all_gather | solution.py:155
  100.6 8.8 copy-start.3
  164.3 11.3 %copy-start.2 = (f32[512,8,1024]{2,0,1:T(8,128)S(1)}, f32[512,8,1024]{2,0,1:T(8,128)}, u32[]{:S(2)}) copy-start(f32[512,8,1024]{2,0,1:T(8,128)} %get-tuple-element.29) | copy-start | bytes 50331652
  187.8 23.3 %all-to-all-start = ((bf16[32,1024,16]{1,2,0:T(8,128)(2,1)}), bf16[32,1024,16]{1,2,0:T(8,128)(2,1)S(1)}, u32[]{:S(2)}, u32[]{:S(2)}) async-start(bf16[32,1024,16]{1,2,0:T(8,128)(2,1)} %broadcast_in_dim.79), calls=%async_computation | async-start | bytes 2097152 | tf_op jit(solution)/shard_map/all_to_all | solution.py:21
  193.1 392.7 %reduce-scatter.2.cloned.1.call-start = ((), (), s32[]{:S(2)}) async-start(), calls=%async_computation.6 | async-start | bytes 17301504 | tf_op jit(solution)/shard_map/reduce_scatter | solution.py:34
  216.0 6.4 copy-start.1
  228.5 465.1 %copy-start.5 = (bf16[256,256]{1,0:T(8,128)(2,1)S(1)}, bf16[256,256]{1,0:T(8,128)(2,1)}, u32[]{:S(2)}) copy-start(bf16[256,256]{1,0:T(8,128)(2,1)} %param.15) | copy-start | bytes 393220
  228.5 479.7 %copy-start.7 = (f32[256]{0:T(256)S(1)}, f32[256]{0:T(256)}, u32[]{:S(2)}) copy-start(f32[256]{0:T(256)} %param.16) | copy-start | bytes 3076
  228.6 444.6 %all-gather.16.cloned.1.call-start = ((), (), s32[]{:S(2)}) async-start(), calls=%async_computation.7 | async-start | bytes 4325376 | tf_op jit(solution)/shard_map/all_gather | solution.py:171
  588.6 197.6 %all-gather.18.cloned.1.call-start = ((), (), s32[]{:S(2)}) async-start(), calls=%async_computation.8 | async-start | bytes 4325376 | tf_op jit(solution)/shard_map/all_gather | solution.py:182
  693.7 99.9 %copy-start.4 = (bf16[256,256]{1,0:T(8,128)(2,1)}, bf16[256,256]{1,0:T(8,128)(2,1)S(1)}, u32[]{:S(2)}) copy-start(bf16[256,256]{1,0:T(8,128)(2,1)S(1)} %get-tuple-element.17) | copy-start | bytes 393220
  793.6 190.4 %copy-start.8 = (f32[1024]{0:T(1024)S(1)}, f32[1024]{0:T(1024)}, u32[]{:S(2)}) copy-start(f32[1024]{0:T(1024)} %param.18) | copy-start | bytes 12292
  793.6 190.4 %all-to-all-start.3 = ((bf16[4,256,8192]{2,1,0:T(8,128)(2,1)}), bf16[4,256,8192]{2,1,0:T(8,128)(2,1)}, u32[]{:S(2)}, u32[]{:S(2)}) async-start(bf16[4,256,8192]{2,1,0:T(8,128)(2,1)} %stack.2), calls=%async_computation.4 | async-start | bytes 33554432 | tf_op jit(solution)/shard_map/all_to_all | solution.py:185
  984.0 17.1 %copy-start.6 = (s32[1024]{0:T(1024)S(1)}, s32[1024]{0:T(1024)}, u32[]{:S(2)}) copy-start(s32[1024]{0:T(1024)} %param.19) | copy-start | bytes 12292
Sparse Core Ops, SparseCore 0:
  11.1 83.0 all-gather.13
  228.7 357.0 reduce-scatter.1
  589.4 83.7 all-gather.15
  709.1 77.0 all-gather.17
